TPU v7x, 256 devices: a whole 4x4x8 slice. The times are simulated.
256 devices in a mesh: sector: 32 (over z, y), term: 8 (over x, core).
Axes of the slice: x: 4, y: 4, z: 8, core: 2. Of those that a mesh axis runs over, the one named last changes fastest.
Arguments:
- wavefunction: bfloat16 [2, 128, 256, 256], P(None, 'sector'), may hold values from -6 to 6
- left_ops: bfloat16 [64, 128, 256, 256], P('term', 'sector'), may hold values from -0.375 to 0.375
- right_ops: bfloat16 [64, 128, 256, 256], P('term', 'sector'), may hold values from -0.046875 to 0.046875
- targets: int32 [64, 128], P('term', 'sector'), may hold values from 0 to 127, as said below
Outputs:
- sigma: bfloat16 [2, 128, 256, 256], P(None, 'sector', 'term')
Inputs may be any that keep to these rules, and one draw needn't show every extreme that they name: In each device block of targets (8 term groups by 4 source blocks, aligned), at most 2 entries fall into any one group of 4 consecutive target blocks (the blocks k * 4 to k * 4 + 3), and some group receives exactly 2 of them.
All inputs are finite; a program needn't handle non-finite values.
Results may differ from a plain program's by a relative error of at most 0.0049.
Values may be sent and summed in bfloat16 or wider, within the bound.
A program may use at most 192 MiB of HBM per device.

v0:
```python
import jax
import jax.numpy as jnp
from jax import lax
from jax.sharding import PartitionSpec as P


def slot_rank(dest_row):
    count = dest_row.shape[0]
    same = dest_row[:, None] == dest_row[None, :]
    lower = jnp.arange(count)[None, :] < jnp.arange(count)[:, None]
    return jnp.sum((same & lower).astype(jnp.int32), axis=1)


def shards(wavefunction, left_ops, right_ops, targets):
    group_dev, sector_dev, width, unused = left_ops.shape
    per_dev = group_dev * sector_dev
    sectors = lax.axis_size("sector")
    capacity = max(2, (2 * per_dev + sectors - 1) // sectors)
    slot_total = sectors * capacity
    my_index = lax.axis_index("sector")
    flat_targets = targets.reshape(per_dev)
    dest_dev = flat_targets // sector_dev
    send_slot = dest_dev * capacity + slot_rank(dest_dev)
    placing = (send_slot[None, :] == jnp.arange(slot_total)[:, None]).astype(jnp.bfloat16)
    halves = jnp.einsum(
        "tsij,vsjk->tsvik", left_ops, wavefunction, preferred_element_type=jnp.float32
    ).astype(jnp.bfloat16)
    send_buf = jnp.dot(
        placing, halves.reshape(per_dev, -1), preferred_element_type=jnp.float32
    ).astype(jnp.bfloat16)
    send_buf = send_buf.reshape(slot_total, 2, width, width)
    received = lax.all_to_all(send_buf, "sector", split_axis=0, concat_axis=0, tiled=True)
    all_targets = lax.all_gather(targets.reshape(1, per_dev), "sector", axis=0, tiled=True)
    all_dest = all_targets // sector_dev
    all_rank = jax.vmap(slot_rank)(all_dest)
    match = (all_dest[:, None, :] == my_index) & (
        all_rank[:, None, :] == jnp.arange(capacity)[None, :, None]
    )
    match_int = match.astype(jnp.int32)
    valid = jnp.sum(match_int, axis=2).reshape(slot_total)
    source_row = jnp.sum(
        match_int * jnp.arange(per_dev, dtype=jnp.int32)[None, None, :], axis=2
    ).reshape(slot_total)
    target_local = (jnp.sum(match_int * all_targets[:, None, :], axis=2) % sector_dev).reshape(
        slot_total
    )
    group_local = source_row // sector_dev
    right_sel = jnp.take(
        right_ops.reshape(per_dev, width, width), group_local * sector_dev + target_local, axis=0
    )
    products = jnp.einsum("rvij,rjk->rvik", received, right_sel, preferred_element_type=jnp.float32)
    owner_pick = (
        (target_local[None, :] == jnp.arange(sector_dev)[:, None]) & (valid[None, :] > 0)
    ).astype(jnp.float32)
    partial_sum = jnp.einsum("cr,rvik->vcik", owner_pick, products, precision=lax.Precision.HIGHEST)
    total = lax.psum(partial_sum, "term")
    row_count = width // lax.axis_size("term")
    result = lax.dynamic_slice_in_dim(total, lax.axis_index("term") * row_count, row_count, 2)
    return result.astype(jnp.bfloat16)


def solution(mesh):
    in_specs = (
        P(None, "sector", None, None),
        P("term", "sector", None, None),
        P("term", "sector", None, None),
        P("term", "sector"),
    )
    out_specs = P(None, "sector", "term", None)
    return jax.shard_map(shards, mesh=mesh, in_specs=in_specs, out_specs=out_specs, check_vma=False)
```

profile of v0, /device:TPU:1, one launch (start us, length us, event | category | flops | bytes accessed | tf_op | source)
XLA Modules:
  0.0 614.9 jit_solution(8608519308723364203)
XLA Ops:
  0.0 0.0 copy-start
  0.0 0.8 copy.23
  0.8 0.1 reshape.284
  0.9 0.2 convert_reduce_fusion.2
  1.1 0.1 copy-done
  1.2 7.9 %convert_bitcast_fusion = bf16[8,4,2,256,256]{3,4,0,2,1:T(8,128)(2,1)} fusion(bf16[8,4,256,256]{3,2,1,0:T(8,128)(2,1)} %param.5, bf16[2,4,256,256]{3,2,1,0:T(8,128)(2,1)S(1)} %copy-done), kind=kOutput, calls=%fused_computation.7 | convolution fusion | flops 2151677952 | bytes 13631488 | tf_op jit(solution)/shard_map/tsij,vsjk->tsvik/dot_general | solution.py:25
  9.1 12.1 %copy.26 = bf16[8,4,2,256,256]{4,3,2,1,0:T(8,128)(2,1)} copy(bf16[8,4,2,256,256]{3,4,0,2,1:T(8,128)(2,1)} %convert_bitcast_fusion) | data formatting | bytes 16777216 | tf_op jit(solution)/shard_map/convert_element_type | solution.py:27
  21.2 8.9 %reshape.285 = bf16[32,131072]{1,0:T(8,128)(2,1)} reshape(bf16[8,4,2,256,256]{4,3,2,1,0:T(8,128)(2,1)} %copy.26) | data formatting | bytes 16777216 | tf_op jit(solution)/shard_map/reshape | solution.py:29
  30.1 11.4 %convolution_convert_fusion = bf16[64,131072]{1,0:T(8,128)(2,1)} fusion(bf16[32,131072]{1,0:T(8,128)(2,1)} %reshape.285, s32[32]{0:T(128)S(1)} %multiply_add_fusion), kind=kOutput, calls=%fused_computation.1 | convolution fusion | flops 545261568 | bytes 25165952 | tf_op jit(solution)/shard_map/dot_general | solution.py:28
  41.5 15.6 %copy.43 = bf16[8,8,512,256]{3,2,1,0:T(8,128)(2,1)} copy(bf16[8,8,512,256]{3,1,2,0:T(8,128)(2,1)} %bitcast.34) | data formatting | bytes 33554432
  57.2 12.2 %all-to-all-start = ((bf16[64,2,256,256]{3,2,1,0:T(8,128)(2,1)}), bf16[64,2,256,256]{3,2,1,0:T(8,128)(2,1)}, u32[]{:S(2)}, u32[]{:S(2)}) async-start(bf16[64,2,256,256]{3,2,1,0:T(8,128)(2,1)} %bitcast.33), calls=%async_computation | async-start | bytes 33554432 | tf_op jit(solution)/shard_map/all_to_all | solution.py:32
  69.4 0.1 reshape.299
  69.4 418.0 %all-gather = s32[32,1,32]{2,1,0:T(1,128)S(1)} all-gather(s32[1,1,32]{2,1,0:T(1,128)S(1)} %reshape.299), channel_id=1, replica_groups=mesh['sector'=32,'term'=8] {'sector'}, dimensions={0}, use_global_device_ids=true | all-gather | bytes 4224 | tf_op jit(solution)/shard_map/all_gather | solution.py:33
  487.5 0.8 convert_reduce_fusion
  488.3 0.2 convert_reduce_fusion.1
  488.5 0.1 copy.29
  488.6 0.1 reduce_sum.54
  488.7 0.1 reduce_sum.53
  488.8 0.1 copy.28
  488.9 0.1 reshape.290
  489.0 0.1 reshape.288
  489.1 0.1 copy.32
  489.2 0.1 gt.13
  489.4 7.8 %gather_fusion = bf16[64,256,256]{2,1,0:T(8,128)(2,1)} fusion(bf16[32,256,256]{2,1,0:T(8,128)(2,1)} %bitcast.35, s32[1024]{0:T(1024)S(1)} %pad_clamp_fusion), kind=kCustom, calls=%fused_computation | custom fusion | bytes 16777472 | tf_op jit(solution)/shard_map/jit(_take)/gather | solution.py:48
  497.2 0.0 all-to-all-done
  497.2 19.7 %fusion.2 = f32[64,2,256,256]{3,2,1,0:T(8,128)} fusion(bf16[64,2,256,256]{3,2,1,0:T(8,128)(2,1)} %all-to-all-done, bf16[64,256,256]{2,1,0:T(8,128)(2,1)} %gather_fusion, pred[64]{0:T(512)(128)(4,1)S(1)} %get-tuple-element.8), kind=kOutput, calls=%fused_computation.4 | convolution fusion | flops 4299161600 | bytes 58720320 | tf_op jit(solution)/shard_map/rvij,rjk->rvik/dot_general | solution.py:51
  516.9 0.0 copy-start.1
  516.9 36.5 %fusion.8 = f32[2,4,256,256]{3,1,2,0:T(4,128)S(1)} fusion(f32[64,2,256,256]{3,2,1,0:T(8,128)} %fusion.2, s32[64]{0:T(128)S(1)} %get-tuple-element.9, pred[64]{0:T(512)(128)(4,1)S(1)} %gt.13), kind=kOutput, calls=%fused_computation.11 | convolution fusion | flops 402653696 | bytes 35651904 | tf_op jit(solution)/shard_map/cr,rvik->vcik/dot_general | solution.py:55
  553.3 59.9 %all-reduce.1 = bf16[2,4,256,256]{3,1,2,0:T(4,128)(2,1)} all-reduce(f32[2,4,256,256]{3,1,2,0:T(4,128)S(1)} %fusion.8), channel_id=1, replica_groups=mesh['sector'=32,'term'=8] {'term'}, use_global_device_ids=true, to_apply=%region_5.6 | all-reduce | flops 524288 | bytes 3145728 | tf_op jit(solution)/shard_map/psum | solution.py:56
  613.2 1.0 dynamic-slice_convert_fusion
  614.2 0.7 copy.34
  614.9 0.0 copy-done.1
  (8 shorter events, 0.1 us)
Async XLA Ops:
  0.0 1.2 copy-start
  57.2 440.0 %all-to-all-start = ((bf16[64,2,256,256]{3,2,1,0:T(8,128)(2,1)}), bf16[64,2,256,256]{3,2,1,0:T(8,128)(2,1)}, u32[]{:S(2)}, u32[]{:S(2)}) async-start(bf16[64,2,256,256]{3,2,1,0:T(8,128)(2,1)} %bitcast.33), calls=%async_computation | async-start | bytes 33554432 | tf_op jit(solution)/shard_map/all_to_all | solution.py:32
  516.9 98.0 %copy-start.1 = (bf16[2,4,256,256]{3,2,1,0:T(8,128)(2,1)S(1)}, bf16[2,4,256,256]{3,2,1,0:T(8,128)(2,1)}, u32[]{:S(2)}) copy-start(bf16[2,4,256,256]{3,2,1,0:T(8,128)(2,1)} %param.4) | copy-start | bytes 3145732
where the time goes:
time: 616 us; the launch traced here: 615 us
  blocking collectives  478 us (78%)
  matrix products  75.4 us (12%)
  local copies, waits for them, and re-layouts  48 us (8%)
  starting transfers between devices  12.2 us (2%)
    all_gather x1, blocking collectives, shards(): lax.all_gather(targets.reshape(1, per_dev), 'sector', axis=0, tiled=True)  418 us
    psum x1, blocking collectives, shards(): total = lax.psum(partial_sum, 'term')  59.9 us
    dot_general x1, matrix products, shards(): jnp.einsum('cr,rvik->vcik', owner_pick, products, precision=lax.Precision...  36.5 us
    dot_general x1, matrix products, shards(): jnp.einsum('rvij,rjk->rvik', received, right_sel, preferred_element_type=...  19.7 us
    unnamed x7, local copies, waits for them, and re-layouts  16.7 us
  transfers between devices with their start and end apart: 1, of which 0 were waited for; matrix products, arithmetic and copies ran while one was open for 2% of the time, Pallas kernels for 0%

commit v1 on v0

v1 whole, which is shorter than its diff:
```python
import jax
import jax.numpy as jnp
from jax import lax
from jax.experimental import pallas as pl
from jax.experimental.pallas import tpu as pltpu
from jax.sharding import PartitionSpec as P


def slot_rank(dest_row):
    count = dest_row.shape[0]
    same = dest_row[:, None] == dest_row[None, :]
    lower = jnp.arange(count)[None, :] < jnp.arange(count)[:, None]
    return jnp.sum((same & lower).astype(jnp.int32), axis=1)


def contract(wave_at, right_at, owner_at, valid, left_ref, wave_ref, right_ref, out_ref, acc):
    step = pl.program_id(0)

    @pl.when(step == 0)
    def _():
        acc[...] = jnp.zeros_like(acc)

    @pl.when(valid[step] > 0)
    def _():
        owner = owner_at[step]
        for v in range(2):
            half = jnp.dot(left_ref[0], wave_ref[v, 0], preferred_element_type=jnp.float32)
            half = half.astype(jnp.bfloat16)
            acc[v, owner] += jnp.dot(half, right_ref[0], preferred_element_type=jnp.float32)

    @pl.when(step == pl.num_programs(0) - 1)
    def _():
        out_ref[...] = acc[...].astype(out_ref.dtype)


def shards(wavefunction, left_ops, right_ops, targets):
    group_dev, sector_dev, width, unused = left_ops.shape
    per_dev = group_dev * sector_dev
    sectors = lax.axis_size("sector")
    terms = lax.axis_size("term")
    capacity = max(2, (2 * per_dev + sectors - 1) // sectors)
    slot_total = sectors * capacity
    my_index = lax.axis_index("sector")
    my_term = lax.axis_index("term")

    share = lax.dynamic_index_in_dim(
        wavefunction.reshape(2 * sector_dev, width, width), my_term, 0, keepdims=True
    )
    share = lax.all_gather(share, "sector", axis=0, tiled=True)
    wave_all = lax.all_gather(share, "term", axis=0, tiled=True)
    wave_all = wave_all.reshape(2, sector_dev * sectors, width, width)

    flat_targets = targets.reshape(per_dev)
    dest_dev = flat_targets // sector_dev
    send_slot = dest_dev * capacity + slot_rank(dest_dev)
    placing = (send_slot[None, :] == jnp.arange(slot_total)[:, None]).astype(jnp.int32)
    send_row = jnp.sum(placing * jnp.arange(per_dev, dtype=jnp.int32)[None, :], axis=1)
    send_buf = jnp.take(left_ops.reshape(per_dev, width, width), send_row, axis=0)
    left_all = lax.all_to_all(send_buf, "sector", split_axis=0, concat_axis=0, tiled=True)

    all_targets = lax.all_gather(targets.reshape(1, per_dev), "sector", axis=0, tiled=True)
    all_dest = all_targets // sector_dev
    all_rank = jax.vmap(slot_rank)(all_dest)
    match = (all_dest[:, None, :] == my_index) & (
        all_rank[:, None, :] == jnp.arange(capacity)[None, :, None]
    )
    match_int = match.astype(jnp.int32)
    valid = jnp.sum(match_int, axis=2).reshape(slot_total)
    source_row = jnp.sum(
        match_int * jnp.arange(per_dev, dtype=jnp.int32)[None, None, :], axis=2
    ).reshape(slot_total)
    owner = (jnp.sum(match_int * all_targets[:, None, :], axis=2) % sector_dev).reshape(slot_total)
    right_at = source_row // sector_dev * sector_dev + owner
    wave_at = source_row % sector_dev * sectors + jnp.arange(slot_total, dtype=jnp.int32) // capacity

    partial = pl.pallas_call(
        contract,
        out_shape=jax.ShapeDtypeStruct((2, sector_dev, width, width), jnp.bfloat16),
        grid_spec=pltpu.PrefetchScalarGridSpec(
            num_scalar_prefetch=4,
            grid=(slot_total,),
            in_specs=[
                pl.BlockSpec((1, width, width), lambda i, w, r, o, u: (i, 0, 0)),
                pl.BlockSpec((2, 1, width, width), lambda i, w, r, o, u: (0, w[i], 0, 0)),
                pl.BlockSpec((1, width, width), lambda i, w, r, o, u: (r[i], 0, 0)),
            ],
            out_specs=pl.BlockSpec((2, sector_dev, width, width), lambda i, w, r, o, u: (0, 0, 0, 0)),
            scratch_shapes=[pltpu.VMEM((2, sector_dev, width, width), jnp.float32)],
        ),
        compiler_params=pltpu.CompilerParams(vmem_limit_bytes=32 << 20),
    )(wave_at, right_at, owner, valid, left_all, wave_all, right_ops.reshape(per_dev, width, width))

    row_count = width // terms
    pieces = partial.reshape(2, sector_dev, terms, row_count, width)
    pieces = lax.all_to_all(pieces, "term", split_axis=2, concat_axis=2, tiled=True)
    return jnp.sum(pieces.astype(jnp.float32), axis=2).astype(jnp.bfloat16)


def solution(mesh):
    in_specs = (
        P(None, "sector", None, None),
        P("term", "sector", None, None),
        P("term", "sector", None, None),
        P("term", "sector"),
    )
    out_specs = P(None, "sector", "term", None)
    return jax.shard_map(shards, mesh=mesh, in_specs=in_specs, out_specs=out_specs, check_vma=False)
```

time: 616 us -> 408 us (0.66)
  blocking collectives: 478 us -> 236 us
  waiting for transfers between devices: 0.01 us -> 84.5 us
  matrix products: 75.4 us -> 0 us
  Pallas kernels: 0 us -> 44.1 us
  local copies, waits for them, and re-layouts: 48 us -> 13.3 us
  between operations: 0.1 us -> 13.5 us
  other arithmetic: 1.24 us -> 10.7 us
  starting transfers between devices: 12.2 us -> 5.04 us
    all_gather x1, blocking collectives: 418 us -> 205 us  [shards(): lax.all_gather(targets.reshape(1, per_dev), 'sector', axis=0, tiled=True)]
    all_gather x0 -> x2, waiting for transfers between devices: none -> 84.5 us  [the longest x1 84.5 us: shards(): share = lax.all_gather(share, 'sector', axis=0, tiled=True)]
    dot_general x4 -> x0, matrix products: 75.4 us -> none  [the longest x1 36.5 us: shards(): jnp.einsum('cr,rvik->vcik', owner_pick, products, precision=lax.Precision...]
    psum x1 -> x0, blocking collectives: 59.9 us -> none  [shards(): total = lax.psum(partial_sum, 'term')]
    pallas_call x0 -> x1, Pallas kernels: none -> 44.1 us  [shards(): pl.pallas_call(contract, out_shape=jax.ShapeDtypeStruct((2, sector_dev, w...]
    all_to_all x0 -> x1, blocking collectives: none -> 30.4 us  [shards(): lax.all_to_all(pieces, 'term', split_axis=2, concat_axis=2, tiled=True)]
    convert_element_type x3 -> x0, local copies, waits for them, and re-layouts: 13.8 us -> none  [the longest x1 12.1 us: shards(): halves = jnp.einsum('tsij,vsjk->tsvik', left_ops, wavefunction, preferred...]
    unnamed x7 -> x8, local copies, waits for them, and re-layouts: 16.7 us -> 4.25 us
  transfers between devices with their start and end apart: 1 -> 3, of which waited for: 0 -> 1; matrix products, arithmetic and copies ran while one was open for 2% -> 5% of each run, Pallas kernels for 0% -> 0%
where the time goes in v1:
time: 408 us; the launch traced here: 407 us
  blocking collectives  236 us (58%)
  waiting for transfers between devices  84.5 us (21%)
  Pallas kernels  44.1 us (11%)
  between operations  13.5 us (3%)
  local copies, waits for them, and re-layouts  13.3 us (3%)
  other arithmetic  10.7 us (3%)
  starting transfers between devices  5.04 us (1%)
    all_gather x1, blocking collectives, shards(): lax.all_gather(targets.reshape(1, per_dev), 'sector', axis=0, tiled=True)  205 us
    all_gather x1, waiting for transfers between devices, shards(): share = lax.all_gather(share, 'sector', axis=0, tiled=True)  84.5 us
    pallas_call x1, Pallas kernels, shards(): pl.pallas_call(contract, out_shape=jax.ShapeDtypeStruct((2, sector_dev, w...  44.1 us
    all_to_all x1, blocking collectives, shards(): lax.all_to_all(pieces, 'term', split_axis=2, concat_axis=2, tiled=True)  30.4 us
    select_n x2, other arithmetic, shards(): jnp.take(left_ops.reshape(per_dev, width, width), send_row, axis=0)  8.58 us
  transfers between devices with their start and end apart: 3, of which 1 were waited for; matrix products, arithmetic and copies ran while one was open for 5% of the time, Pallas kernels for 0%

profile of v1, /device:TPU:1, one launch (start us, length us, event | category | flops | bytes accessed | tf_op | source)
XLA Modules:
  0.0 407.1 jit_solution(8226409225203431304)
XLA Ops:
  6.5 0.0 copy-start
  6.5 1.2 copy-done
  7.8 0.7 constant_dynamic-slice_fusion
  8.4 0.0 all-gather.4.cloned.1.call-update
  8.4 0.0 all-gather.6.cloned.1.call-start
  8.5 84.5 %all-gather.4.cloned.1.call-done = bf16[32,256,256]{2,1,0:T(8,128)(2,1)} async-done(((bf16[1,256,256]{2,1,0:T(8,128)(2,1)}), bf16[32,256,256]{2,1,0:T(8,128)(2,1)}) %all-gather.4.cloned.1.call-update) | async-done | bytes 4194320 | tf_op jit(solution)/shard_map/all_gather | solution.py:49
  93.0 0.0 all-gather.6.cloned.1.call-update
  93.0 0.8 copy.12
  93.8 0.1 reshape.137
  93.9 0.2 convert_reduce_fusion.2
  94.1 0.1 select_reduce_fusion.2
  94.2 7.6 %gather_fusion = bf16[64,256,256]{2,1,0:T(8,128)(2,1)} fusion(bf16[32,256,256]{2,1,0:T(8,128)(2,1)} %bitcast.14, s32[1024]{0:T(1024)S(1)} %pad_clamp_fusion), kind=kCustom, calls=%fused_computation | custom fusion | bytes 16777472 | tf_op jit(solution)/shard_map/jit(_take)/gather | solution.py:58
  101.8 8.6 %broadcast_select_fusion = bf16[64,256,256]{2,1,0:T(8,128)(2,1)} fusion(bf16[64,256,256]{2,1,0:T(8,128)(2,1)} %gather_fusion, pred[64]{0:T(512)(128)(4,1)S(1)} %compare_and_fusion), kind=kLoop, calls=%fused_computation.1 | loop fusion | flops 4194304 | bytes 16777280 | tf_op jit(solution)/shard_map/jit(_take)/select_n | solution.py:58
  110.4 5.0 %all-to-all-start = ((bf16[64,256,256]{2,1,0:T(8,128)(2,1)}), bf16[64,256,256]{2,1,0:T(8,128)(2,1)}, u32[]{:S(2)}, u32[]{:S(2)}) async-start(bf16[64,256,256]{2,1,0:T(8,128)(2,1)} %broadcast_select_fusion), calls=%async_computation | async-start | bytes 16777216 | tf_op jit(solution)/shard_map/all_to_all | solution.py:59
  115.4 0.1 reshape.151
  115.5 205.5 %all-gather = s32[32,1,32]{2,1,0:T(1,128)S(1)} all-gather(s32[1,1,32]{2,1,0:T(1,128)S(1)} %reshape.151), channel_id=1, replica_groups=mesh['sector'=32,'term'=8] {'sector'}, dimensions={0}, use_global_device_ids=true | all-gather | bytes 4224 | tf_op jit(solution)/shard_map/all_gather | solution.py:61
  321.0 0.8 convert_reduce_fusion
  321.7 0.2 convert_reduce_fusion.1
  321.9 0.1 copy.14
  322.0 0.1 reduce_sum.73
  322.1 0.1 copy.13
  322.2 0.1 reshape.135
  322.3 0.1 copy.15
  322.4 0.1 reshape.136.valid
  322.6 0.0 all-to-all-done.left_ref
  322.6 0.0 all-gather.6.cloned.1.call-done
  322.6 0.0 copy-start.2
  322.6 2.2 copy-done.2
  324.8 44.1 %shard_map.46 = bf16[2,4,256,256]{3,2,1,0:T(8,128)(2,1)S(1)} custom-call(s32[64]{0:T(128)S(1)} %get-tuple-element.12.wave_at, s32[64]{0:T(128)S(1)} %get-tuple-element.8.right_at, s32[64]{0:T(128)S(1)} %get-tuple-element.9.owner_at, s32[64]{0:T(128)S(1)} %reshape.136.valid, bf16[64,256,256]{2,1,0:T(8,128)(2,1)} %all-to-all-done.left_ref, ...), custom_call_target="tpu_custom_call" | custom-call | tf_op jit(solution)/shard_map/pallas_call | solution.py:76
  368.9 0.1 copy.17
  369.0 30.4 %all_to_all.10 = bf16[2,4,8,32,256]{4,3,1,0,2:T(8,128)(2,1)S(1)} all-to-all(bf16[2,4,8,32,256]{4,3,1,0,2:T(8,128)(2,1)S(1)} %copy.17), channel_id=1, replica_groups=mesh['sector'=32,'term'=8] {'term'}, dimensions={2} | all-to-all | bytes 2097152 | tf_op jit(solution)/shard_map/all_to_all | solution.py:95
  399.4 0.8 reduce_sum.78
  (11 shorter events, 0.1 us)
Async XLA Ops:
  6.5 1.2 copy-start
  6.5 86.4 %all-gather.4.cloned.1.call-start = ((), (), s32[]{:S(2)}) async-start(), calls=%async_computation.2 | async-start | bytes 4325376 | tf_op jit(solution)/shard_map/all_gather | solution.py:49
  8.4 314.1 %all-gather.6.cloned.1.call-start = ((), (), s32[]{:S(2)}) async-start(), calls=%async_computation.3 | async-start | bytes 37748736 | tf_op jit(solution)/shard_map/all_gather | solution.py:50
  110.4 212.2 %all-to-all-start = ((bf16[64,256,256]{2,1,0:T(8,128)(2,1)}), bf16[64,256,256]{2,1,0:T(8,128)(2,1)}, u32[]{:S(2)}, u32[]{:S(2)}) async-start(bf16[64,256,256]{2,1,0:T(8,128)(2,1)} %broadcast_select_fusion), calls=%async_computation | async-start | bytes 16777216 | tf_op jit(solution)/shard_map/all_to_all | solution.py:59
  322.6 2.2 copy-start.2
  324.8 75.5 %copy-start.1 = (bf16[2,4,256,256]{3,2,1,0:T(8,128)(2,1)S(1)}, bf16[2,4,256,256]{3,2,1,0:T(8,128)(2,1)}, u32[]{:S(2)}) copy-start(bf16[2,4,256,256]{3,2,1,0:T(8,128)(2,1)} %param.4) | copy-start | bytes 3145732
Sparse Core Ops, SparseCore 0:
  9.9 82.9 all-gather.3
  94.8 158.7 all-gather.5

commit v2 on v1

--- a/solution.py
+++ b/solution.py
@@ -1,3 +1,5 @@
+import functools
+
 import jax
 import jax.numpy as jnp
 from jax import lax
@@ -5,12 +7,156 @@
 from jax.experimental.pallas import tpu as pltpu
 from jax.sharding import PartitionSpec as P
 
+MESH = pl.DeviceIdType.MESH
+NZ, NY, NX = 8, 4, 4
+STEPS = [(dz, dy) for dy in (0, -1, 1, 2) for dz in (0, 4, 2, -2, 1, -1, 3, -3)]
+ROWS = (0, 1, -1, 2)
+WINDOW = 8
+
 
 def slot_rank(dest_row):
     count = dest_row.shape[0]
     same = dest_row[:, None] == dest_row[None, :]
     lower = jnp.arange(count)[None, :] < jnp.arange(count)[:, None]
     return jnp.sum((same & lower).astype(jnp.int32), axis=1)
+
+
+def place():
+    sector, term = lax.axis_index("sector"), lax.axis_index("term")
+    return sector // NY, lax.rem(sector, NY), term // 2, lax.rem(term, 2)
+
+
+def shift(index, by, size):
+    return lax.rem(index + by + size, size)
+
+
+def exchange(send_row, left_ref, wave_ref, recv_ref, all_ref, send, own_sem, a2a_s, a2a_r, ring_s, ring_r,
+             row_s, row_r, col_s, col_r, hand_s, hand_r, core_s, core_r):
+    z, y, x, c = place()
+
+    def device(dz=0, dy=0, dx=0, dc=0):
+        return (shift(z, dz, NZ) * NY + shift(y, dy, NY), shift(x, dx, NX) * 2 + lax.rem(c + dc, 2))
+
+    def term(dx):
+        return shift(x, dx, NX) * 2 + c
+
+    barrier = pltpu.get_barrier_semaphore()
+    partners = [device(dz, dy) for dz, dy in STEPS[1:]] + [device(dx=1), device(dx=-1), device(dc=1)]
+    for partner in partners:
+        pl.semaphore_signal(barrier, inc=1, device_id=partner, device_id_type=MESH)
+    pl.semaphore_wait(barrier, len(partners))
+
+    def remote(src, dst, sems, where):
+        copy = pltpu.make_async_remote_copy(src, dst, *sems, device_id=where, device_id_type=MESH)
+        copy.start()
+        return copy
+
+    mine = x * 2 + c
+    own = pltpu.make_async_copy(wave_ref.at[mine], all_ref.at[mine, y, z], own_sem.at[0])
+    own.start()
+
+    ring = {}
+
+    def ring_step(sign, hop):
+        k = hop - 1 + (4 if sign < 0 else 0)
+        spot = all_ref.at[mine, y, shift(z, -sign * (hop - 1), NZ)]
+        src = wave_ref.at[mine] if hop == 1 else spot
+        ring[sign, hop] = remote(src, spot, (ring_s.at[k], ring_r.at[k]), device(dz=sign))
+
+    a2a = []
+
+    def send_left(k):
+        dz, dy = STEPS[k]
+        to = shift(z, dz, NZ) * NY + shift(y, dy, NY)
+        for r in range(2):
+            send[k, r] = left_ref[send_row[to * 2 + r]]
+        if k == 0:
+            copy = pltpu.make_async_copy(send.at[0], recv_ref.at[0], own_sem.at[1])
+            copy.start()
+        else:
+            copy = remote(send.at[k], recv_ref.at[k], (a2a_s.at[k], a2a_r.at[k]), device(dz, dy))
+        a2a.append(copy)
+
+    def paced(k):
+        if k > WINDOW:
+            a2a[k - WINDOW].wait_send()
+        send_left(k)
+
+    ring_step(1, 1)
+    ring_step(-1, 1)
+    for k in range(4):
+        send_left(k)
+    for hop in (2, 3, 4):
+        ring[1, hop - 1].wait_recv()
+        ring_step(1, hop)
+        if hop < 4:
+            ring[-1, hop - 1].wait_recv()
+            ring_step(-1, hop)
+    ring[1, 4].wait_recv()
+    ring[-1, 3].wait_recv()
+    own.wait()
+
+    rows, cols, hands, cores = [], [], [], []
+    for i, dy in enumerate(ROWS[1:]):
+        rows.append(remote(all_ref.at[mine, y], all_ref.at[mine, y], (row_s.at[i], row_r.at[i]), device(dy=-dy)))
+
+    def along(q):
+        if q:
+            rows[q - 1].wait_recv()
+        line = shift(y, ROWS[q], NY)
+        for i, dx in enumerate((1, -1)):
+            spot = all_ref.at[mine, line]
+            cols.append(remote(spot, spot, (col_s.at[q, i], col_r.at[q, i]), device(dx=dx)))
+
+    def hand_on(q):
+        line = shift(y, ROWS[q], NY)
+        for i, dx in enumerate((1, -1)):
+            cols[2 * q + i].wait_recv()
+            spot = all_ref.at[term(-dx), line, pl.ds(4 * i, 4)]
+            hands.append(remote(spot, spot, (hand_s.at[q, i], hand_r.at[q, i]), device(dx=dx)))
+
+    def across(q):
+        line = shift(y, ROWS[q], NY)
+        for i in range(2):
+            hands[2 * q + i].wait_recv()
+        for dx in range(NX):
+            spot = all_ref.at[term(dx), line]
+            cores.append(remote(spot, spot, (core_s.at[q, dx], core_r.at[q, dx]), device(dc=1)))
+
+    along(0)
+    for k in range(4, 12):
+        paced(k)
+    along(1)
+    for k in range(12, 16):
+        paced(k)
+    along(2)
+    hand_on(0)
+    for k in range(16, 20):
+        paced(k)
+    along(3)
+    across(0)
+    hand_on(1)
+    for k in range(20, 24):
+        paced(k)
+    across(1)
+    hand_on(2)
+    for k in range(24, 28):
+        paced(k)
+    across(2)
+    hand_on(3)
+    for k in range(28, 32):
+        paced(k)
+    across(3)
+
+    for copy in cores:
+        copy.wait()
+    for copy in [*rows, *cols, *hands, *ring.values()]:
+        copy.wait_send()
+    a2a[0].wait()
+    for k in range(1, 32):
+        if k > 31 - WINDOW:
+            a2a[k].wait_send()
+        a2a[k].wait_recv()
 
 
 def contract(wave_at, right_at, owner_at, valid, left_ref, wave_ref, right_ref, out_ref, acc):
@@ -38,27 +184,22 @@
     per_dev = group_dev * sector_dev
     sectors = lax.axis_size("sector")
     terms = lax.axis_size("term")
-    capacity = max(2, (2 * per_dev + sectors - 1) // sectors)
+    capacity = 2
     slot_total = sectors * capacity
     my_index = lax.axis_index("sector")
-    my_term = lax.axis_index("term")
-
-    share = lax.dynamic_index_in_dim(
-        wavefunction.reshape(2 * sector_dev, width, width), my_term, 0, keepdims=True
-    )
-    share = lax.all_gather(share, "sector", axis=0, tiled=True)
-    wave_all = lax.all_gather(share, "term", axis=0, tiled=True)
-    wave_all = wave_all.reshape(2, sector_dev * sectors, width, width)
+    z, y, x, c = place()
 
     flat_targets = targets.reshape(per_dev)
+    all_targets = lax.all_gather(targets.reshape(1, per_dev), "sector", axis=0, tiled=True)
     dest_dev = flat_targets // sector_dev
     send_slot = dest_dev * capacity + slot_rank(dest_dev)
     placing = (send_slot[None, :] == jnp.arange(slot_total)[:, None]).astype(jnp.int32)
     send_row = jnp.sum(placing * jnp.arange(per_dev, dtype=jnp.int32)[None, :], axis=1)
-    send_buf = jnp.take(left_ops.reshape(per_dev, width, width), send_row, axis=0)
-    left_all = lax.all_to_all(send_buf, "sector", split_axis=0, concat_axis=0, tiled=True)
-
-    all_targets = lax.all_gather(targets.reshape(1, per_dev), "sector", axis=0, tiled=True)
+
+    steps = jnp.array(STEPS, jnp.int32)
+    source = shift(z, -steps[:, 0], NZ) * NY + shift(y, -steps[:, 1], NY)
+    pick = (source[:, None] == jnp.arange(sectors)[None, :]).astype(jnp.int32)
+    all_targets = jnp.sum(pick[:, :, None] * all_targets[None], axis=1)
     all_dest = all_targets // sector_dev
     all_rank = jax.vmap(slot_rank)(all_dest)
     match = (all_dest[:, None, :] == my_index) & (
@@ -71,7 +212,36 @@
     ).reshape(slot_total)
     owner = (jnp.sum(match_int * all_targets[:, None, :], axis=2) % sector_dev).reshape(slot_total)
     right_at = source_row // sector_dev * sector_dev + owner
-    wave_at = source_row % sector_dev * sectors + jnp.arange(slot_total, dtype=jnp.int32) // capacity
+    spot = lax.rem(source, NY) * NZ + source // NY
+    wave_at = source_row % sector_dev * sectors + jnp.repeat(spot, capacity)
+
+    block = (width, width)
+    hbm = pl.BlockSpec(memory_space=pl.ANY)
+    dma = pltpu.SemaphoreType.DMA
+    left_all, wave_all = pl.pallas_call(
+        exchange,
+        out_shape=(
+            jax.ShapeDtypeStruct((sectors, capacity, *block), jnp.bfloat16),
+            jax.ShapeDtypeStruct((terms, NY, NZ, *block), jnp.bfloat16),
+        ),
+        in_specs=[
+            pl.BlockSpec(memory_space=pltpu.SMEM),
+            pl.BlockSpec(memory_space=pltpu.VMEM),
+            hbm,
+        ],
+        out_specs=(hbm, hbm),
+        scratch_shapes=[
+            pltpu.VMEM((sectors, capacity, *block), jnp.bfloat16),
+            dma((2,)),
+            dma((32,)), dma((32,)), dma((8,)), dma((8,)), dma((3,)), dma((3,)),
+            dma((4, 2)), dma((4, 2)), dma((4, 2)), dma((4, 2)), dma((4, 4)), dma((4, 4)),
+        ],
+        compiler_params=pltpu.CompilerParams(
+            collective_id=0, has_side_effects=True, vmem_limit_bytes=40 << 20
+        ),
+    )(send_row, left_ops.reshape(per_dev, *block), wavefunction.reshape(2 * sector_dev, *block))
+    left_all = left_all.reshape(slot_total, *block)
+    wave_all = wave_all.reshape(2, sector_dev * sectors, *block)
 
     partial = pl.pallas_call(
         contract,
@@ -88,7 +258,7 @@
             scratch_shapes=[pltpu.VMEM((2, sector_dev, width, width), jnp.float32)],
         ),
         compiler_params=pltpu.CompilerParams(vmem_limit_bytes=32 << 20),
-    )(wave_at, right_at, owner, valid, left_all, wave_all, right_ops.reshape(per_dev, width, width))
+    )(wave_at, right_at, owner, valid, left_all, wave_all, right_ops.reshape(per_dev, *block))
 
     row_count = width // terms
     pieces = partial.reshape(2, sector_dev, terms, row_count, width)

time: 408 us -> 356 us (0.87)
  the two profiles are of different devices: /device:TPU:1 before, /device:TPU:120 now
where the time goes in v2:
time: 356 us; the launch traced here: 355 us
  Pallas kernels  274 us (77%)
  blocking collectives  69.6 us (20%)
  local copies, waits for them, and re-layouts  7.36 us (2%)
  other arithmetic  3.81 us (1%)
    pallas_call x1, Pallas kernels, shards(): pl.pallas_call(exchange, out_shape=(jax.ShapeDtypeStruct((sectors, capaci...  235 us
    pallas_call x1, Pallas kernels, shards(): pl.pallas_call(contract, out_shape=jax.ShapeDtypeStruct((2, sector_dev, w...  39.3 us
    all_gather x1, blocking collectives, shards(): lax.all_gather(targets.reshape(1, per_dev), 'sector', axis=0, tiled=True)  37.3 us
    all_to_all x1, blocking collectives, shards(): lax.all_to_all(pieces, 'term', split_axis=2, concat_axis=2, tiled=True)  32.3 us

profile of v2, /device:TPU:120, one launch (start us, length us, event | category | flops | bytes accessed | tf_op | source)
XLA Modules:
  0.0 354.7 jit_solution(6272207161662774144)
XLA Ops:
  0.0 0.7 multiply_add_fusion.2
  0.7 0.7 fusion.15
  1.4 0.8 copy.13
  2.1 0.1 reshape.194
  2.2 0.1 reshape.201
  2.3 0.2 convert_reduce_fusion.2
  2.5 0.1 select_reduce_fusion.2.send_row
  2.6 37.3 %all-gather = s32[32,1,32]{2,1,0:T(1,128)S(1)} all-gather(s32[1,1,32]{2,1,0:T(1,128)S(1)} %reshape.201), channel_id=1, replica_groups=mesh['sector'=32,'term'=8] {'sector'}, dimensions={0}, use_global_device_ids=true | all-gather | bytes 4224 | tf_op jit(solution)/shard_map/all_gather | solution.py:193
  39.9 0.1 fusion.2
  39.9 0.1 broadcast_in_dim.2
  40.0 0.1 reshape.192
  40.1 0.2 multiply_reduce_fusion
  40.4 0.8 convert_reduce_fusion
  41.2 0.2 convert_reduce_fusion.1
  41.3 0.1 copy.16
  41.4 0.1 reshape.193.valid
  41.6 0.1 copy.15
  41.6 0.1 reduce_sum.81
  41.7 0.1 copy.14
  41.8 0.1 reshape.191
  42.0 0.0 copy-start.1
  42.0 2.2 copy-done.1
  44.2 0.0 copy-start.2
  44.2 1.2 copy-done.2
  45.4 234.5 %shard_map.55 = (bf16[32,2,256,256]{3,2,1,0:T(8,128)(2,1)S(1)}, bf16[8,4,8,256,256]{4,3,2,1,0:T(8,128)(2,1)}) custom-call(s32[64]{0:T(128)S(1)} %select_reduce_fusion.2.send_row, bf16[32,256,256]{2,1,0:T(8,128)(2,1)S(1)} %bitcast.20, bf16[8,256,256]{2,1,0:T(8,128)(2,1)S(1)} %bitcast.21), custom_call_target="tpu_custom_call" | custom-call | tf_op jit(solution)/shard_map/pallas_call | solution.py:221
  279.9 0.0 copy-start
  279.9 2.2 copy-done
  282.1 39.3 %shard_map.56 = bf16[2,4,256,256]{3,2,1,0:T(8,128)(2,1)S(1)} custom-call(s32[64]{0:T(128)S(1)} %get-tuple-element.16.wave_at, s32[64]{0:T(128)S(1)} %get-tuple-element.12.right_at, s32[64]{0:T(128)S(1)} %get-tuple-element.13.owner_at, s32[64]{0:T(128)S(1)} %reshape.193.valid, bf16[64,256,256]{2,1,0:T(8,128)(2,1)S(1)} %bitcast.17, ...), custom_call_target="tpu_custom_call" | custom-call | tf_op jit(solution)/shard_map/pallas_call | solution.py:246
  321.5 0.1 copy.18
  321.5 32.3 %all_to_all.5 = bf16[2,4,8,32,256]{4,3,1,0,2:T(8,128)(2,1)S(1)} all-to-all(bf16[2,4,8,32,256]{4,3,1,0,2:T(8,128)(2,1)S(1)} %copy.18), channel_id=1, replica_groups=mesh['sector'=32,'term'=8] {'term'}, dimensions={2} | all-to-all | bytes 2097152 | tf_op jit(solution)/shard_map/all_to_all | solution.py:265
  353.9 0.8 reduce_sum.85
  (5 shorter events, 0.1 us)
Async XLA Ops:
  42.0 2.2 copy-start.1
  44.2 1.2 copy-start.2
  279.9 2.2 copy-start

commit v3 on v2

v3 whole, which is shorter than its diff:
```python
import jax
import jax.numpy as jnp
from jax import lax
from jax.experimental import pallas as pl
from jax.experimental.pallas import tpu as pltpu
from jax.sharding import PartitionSpec as P

MESH = pl.DeviceIdType.MESH
NZ, NY, NX = 8, 4, 4
STEPS = [(dz, dy) for dy in (0, -1, 1, 2) for dz in (0, 4, 2, -2, 1, -1, 3, -3)]
ROWS = (0, 1, -1, 2)
WINDOW = 8


def slot_rank(dest_row):
    count = dest_row.shape[0]
    same = dest_row[:, None] == dest_row[None, :]
    lower = jnp.arange(count)[None, :] < jnp.arange(count)[:, None]
    return jnp.sum((same & lower).astype(jnp.int32), axis=1)


def place():
    sector, term = lax.axis_index("sector"), lax.axis_index("term")
    return sector // NY, lax.rem(sector, NY), term // 2, lax.rem(term, 2)


def shift(index, by, size):
    return lax.rem(index + by + size, size)


def contract_all(code_ref, meta_ref, left_ref, right_ref, wave_ref, out_ref, all_ref, send, recv, meta_got, meta_at, stage, halves,
                 picked, acc, pair, half_sum, got, own_sem, stage_sem, a2a_s, a2a_r, meta_s, meta_r, ring_s, ring_r,
                 row_s, row_r, col_s, col_r, hand_s, hand_r, core_s, core_r, pair_s, pair_r, sum_s, sum_r):
    z, y, x, c = place()
    width = left_ref.shape[-1]

    def device(dz=0, dy=0, dx=0, dc=0):
        return (shift(z, dz, NZ) * NY + shift(y, dy, NY), shift(x, dx, NX) * 2 + lax.rem(c + dc, 2))

    def term(dx):
        return shift(x, dx, NX) * 2 + c

    barrier = pltpu.get_barrier_semaphore()
    partners = [device(dz, dy) for dz, dy in STEPS[1:]] + [device(dx=dx) for dx in (1, -1, 2)] + [device(dc=1)]
    for partner in partners:
        pl.semaphore_signal(barrier, inc=1, device_id=partner, device_id_type=MESH)
    pl.semaphore_wait(barrier, len(partners))

    def remote(src, dst, sems, where):
        copy = pltpu.make_async_remote_copy(src, dst, *sems, device_id=where, device_id_type=MESH)
        copy.start()
        return copy

    mine = x * 2 + c
    own = pltpu.make_async_copy(wave_ref.at[mine], all_ref.at[mine, y, z], own_sem.at[0])
    own.start()

    ring = {}

    def ring_step(sign, hop):
        k = hop - 1 + (4 if sign < 0 else 0)
        spot = all_ref.at[mine, y, shift(z, -sign * (hop - 1), NZ)]
        src = wave_ref.at[mine] if hop == 1 else spot
        ring[sign, hop] = remote(src, spot, (ring_s.at[k], ring_r.at[k]), device(dz=sign))

    a2a = []
    metas = []

    def owner_of(k):
        dz, dy = STEPS[k]
        return shift(z, dz, NZ) * NY + shift(y, dy, NY)

    def send_meta(k):
        src, dst = meta_ref.at[owner_of(k)], meta_got.at[k]
        if k == 0:
            copy = pltpu.make_async_copy(src, dst, own_sem.at[1])
            copy.start()
        else:
            copy = remote(src, dst, (meta_s.at[k], meta_r.at[k]), device(*STEPS[k]))
        metas.append(copy)

    def send_left(k):
        to = owner_of(k)
        buf = recv if k == 0 else send
        for r in range(2):
            buf[k, r] = left_ref[code_ref[to, 0, r] // 8]
        a2a.append(k and remote(send.at[k], recv.at[k], (a2a_s.at[k], a2a_r.at[k]), device(*STEPS[k])))

    def paced(first, last):
        for k in range(first, last):
            if k > WINDOW:
                a2a[k - WINDOW].wait_send()
            send_left(k)

    ring_step(1, 1)
    ring_step(-1, 1)
    for k in range(4):
        send_left(k)
    for k in range(32):
        send_meta(k)
    acc[...] = jnp.zeros_like(acc)
    for hop in (2, 3, 4):
        ring[1, hop - 1].wait_recv()
        ring_step(1, hop)
        if hop < 4:
            ring[-1, hop - 1].wait_recv()
            ring_step(-1, hop)
    ring[1, 4].wait_recv()
    ring[-1, 3].wait_recv()
    own.wait()

    rows, cols, hands, cores = [], [], [], []
    for i, dy in enumerate(ROWS[1:]):
        rows.append(remote(all_ref.at[mine, y], all_ref.at[mine, y], (row_s.at[i], row_r.at[i]), device(dy=-dy)))

    def along(q):
        if q:
            rows[q - 1].wait_recv()
        line = shift(y, ROWS[q], NY)
        for i, dx in enumerate((1, -1)):
            spot = all_ref.at[mine, line]
            cols.append(remote(spot, spot, (col_s.at[q, i], col_r.at[q, i]), device(dx=dx)))

    def hand_on(q):
        line = shift(y, ROWS[q], NY)
        for i, dx in enumerate((1, -1)):
            cols[2 * q + i].wait_recv()
            spot = all_ref.at[term(-dx), line, pl.ds(4 * i, 4)]
            hands.append(remote(spot, spot, (hand_s.at[q, i], hand_r.at[q, i]), device(dx=dx)))

    def across(q):
        line = shift(y, ROWS[q], NY)
        for i in range(2):
            hands[2 * q + i].wait_recv()
        for dx in range(NX):
            spot = all_ref.at[term(dx), line]
            cores.append(remote(spot, spot, (core_s.at[q, dx], core_r.at[q, dx]), device(dc=1)))

    def group(g):
        if g % 2 == 0:
            for copy in cores[2 * g : 2 * g + 4]:
                copy.wait_recv()
        loads = []
        for i in range(4):
            dz, dy = STEPS[4 * g + i]
            copy = pltpu.make_async_copy(all_ref.at[:, shift(y, -dy, NY), shift(z, -dz, NZ)], stage.at[i], stage_sem.at[i])
            copy.start()
            loads.append(copy)
        for copy in loads:
            copy.wait()
        for k in range(max(4 * g, 1), 4 * g + 4):
            a2a[k].wait_recv()

        def slot(j, carry):
            i, r = j // 2, lax.rem(j, 2)
            code = meta_at[4 * g + i, 0, r]
            live, owner, source = lax.rem(code, 2), lax.rem(code // 2, 4), lax.rem(code // 8, 4)
            left = recv[4 * g + i, r]
            span = pl.ds(pl.multiple_of(j * width, width), width)
            for v in range(2):
                half = jnp.dot(left, stage[i, v * 4 + source], preferred_element_type=jnp.float32)
                halves[v * width : (v + 1) * width, span] = half.astype(halves.dtype)
            right = right_ref[code // 32 * 4 + owner]
            for b in range(4):
                keep = (live > 0) & (owner == b)
                picked[b, span, :] = jnp.where(keep, right, jnp.zeros_like(right))
            return carry

        def block(b, carry):
            product = jnp.dot(halves[...], picked[b], preferred_element_type=jnp.float32)
            for v in range(2):
                for t in range(8):
                    at = v * width + t * 32
                    acc[t % 2, t // 2, v, b] += product[at : at + 32]
            return carry

        lax.fori_loop(0, 8, slot, 0)
        lax.fori_loop(0, 4, block, 0)

    along(0)
    paced(4, 12)
    for copy in metas:
        copy.wait() if copy is metas[0] else copy.wait_recv()
    table = pltpu.make_async_copy(meta_got, meta_at, own_sem.at[2])
    table.start()
    along(1)
    paced(12, 16)
    along(2)
    hand_on(0)
    paced(16, 20)
    along(3)
    across(0)
    hand_on(1)
    paced(20, 24)
    across(1)
    table.wait()
    group(0)
    hand_on(2)
    paced(24, 26)
    group(1)
    paced(26, 28)
    across(2)
    group(2)
    hand_on(3)
    paced(28, 30)
    group(3)
    paced(30, 32)
    across(3)
    for g in range(4, 8):
        group(g)

    order = (1, -1, 2, 0)
    pairs, sums = [], []
    for i, dx in enumerate(order):
        pairs.append(remote(acc.at[1 - c, shift(x, dx, NX)], pair.at[i], (pair_s.at[i], pair_r.at[i]), device(dc=1)))
    for i, dx in enumerate(order[:3]):
        pairs[i].wait_recv()
        half_sum[i] = (acc[c, shift(x, dx, NX)] + pair[i]).astype(half_sum.dtype)
        sums.append(remote(half_sum.at[i], got.at[i], (sum_s.at[i], sum_r.at[i]), device(dx=dx)))
    pairs[3].wait_recv()
    total = acc[c, x] + pair[3]
    for i in range(3):
        sums[i].wait_recv()
        total += got[i].astype(jnp.float32)
    out_ref[...] = total.astype(out_ref.dtype)

    for copy in [*rows, *cols, *hands, *cores, *ring.values(), *metas[1:], *a2a[32 - WINDOW :], *pairs, *sums]:
        copy.wait_send()


def shards(wavefunction, left_ops, right_ops, targets):
    group_dev, sector_dev, width, unused = left_ops.shape
    per_dev = group_dev * sector_dev
    sectors = lax.axis_size("sector")
    terms = lax.axis_size("term")
    capacity = 2

    flat_targets = targets.reshape(per_dev)
    dest_dev = flat_targets // sector_dev
    send_slot = dest_dev * capacity + slot_rank(dest_dev)
    lane = jnp.arange(sectors * capacity)
    code = (jnp.arange(per_dev, dtype=jnp.int32) * 4 + flat_targets % sector_dev) * 2 + 1
    code = jnp.sum(jnp.where(send_slot[None, :] == lane[:, None], code[None, :], 0), axis=1)
    code = jnp.pad(code.reshape(sectors, 1, capacity), ((0, 0), (0, 0), (0, 128 - capacity)))

    block = (width, width)
    hbm = pl.BlockSpec(memory_space=pl.ANY)
    vmem = pl.BlockSpec(memory_space=pltpu.VMEM)
    dma = pltpu.SemaphoreType.DMA
    low, wide = jnp.bfloat16, jnp.float32
    piece = (2, sector_dev, width // terms, width)
    out, unused = pl.pallas_call(
        contract_all,
        out_shape=(
            jax.ShapeDtypeStruct(piece, low),
            jax.ShapeDtypeStruct((terms, NY, NZ, *block), low),
        ),
        in_specs=[pl.BlockSpec(memory_space=pltpu.SMEM), vmem, vmem, vmem, hbm],
        out_specs=(vmem, hbm),
        scratch_shapes=[
            pltpu.VMEM((sectors, capacity, *block), low),
            pltpu.VMEM((sectors, capacity, *block), low),
            pltpu.VMEM((sectors, 1, 128), jnp.int32),
            pltpu.SMEM((sectors, 1, 128), jnp.int32),
            pltpu.VMEM((4, terms, *block), low),
            pltpu.VMEM((2 * width, 8 * width), low),
            pltpu.VMEM((4, 8 * width, width), low),
            pltpu.VMEM((2, NX, *piece), wide),
            pltpu.VMEM((NX, *piece), wide),
            pltpu.VMEM((3, *piece), low),
            pltpu.VMEM((3, *piece), low),
            dma((3,)), dma((4,)),
            dma((32,)), dma((32,)), dma((32,)), dma((32,)), dma((8,)), dma((8,)), dma((3,)), dma((3,)),
            dma((4, 2)), dma((4, 2)), dma((4, 2)), dma((4, 2)), dma((4, 4)), dma((4, 4)),
            dma((4,)), dma((4,)), dma((3,)), dma((3,)),
        ],
        compiler_params=pltpu.CompilerParams(
            collective_id=0, has_side_effects=True, vmem_limit_bytes=56 << 20
        ),
    )(
        code, code, left_ops.reshape(per_dev, *block), right_ops.reshape(per_dev, *block),
        wavefunction.reshape(2 * sector_dev, *block),
    )
    return out


def solution(mesh):
    in_specs = (
        P(None, "sector", None, None),
        P("term", "sector", None, None),
        P("term", "sector", None, None),
        P("term", "sector"),
    )
    out_specs = P(None, "sector", "term", None)
    return jax.shard_map(shards, mesh=mesh, in_specs=in_specs, out_specs=out_specs, check_vma=False)
```

time: 356 us -> 289 us (0.81)
  the two profiles are of different devices: /device:TPU:120 before, /device:TPU:243 now
where the time goes in v3:
time: 289 us
  Pallas kernels  286 us (99%)
  local copies, waits for them, and re-layouts  3.13 us (1%)
    pallas_call x1, Pallas kernels, shards(): pl.pallas_call(contract_all, out_shape=(jax.ShapeDtypeStruct(piece, low),...  286 us

profile of v3, /device:TPU:243, one launch (start us, length us, event | category | flops | bytes accessed | tf_op | source)
XLA Modules:
  0.0 289.1 jit_solution(17295436502345234329)
XLA Ops:
  0.0 0.8 copy.9
  0.8 0.1 reshape.112
  0.9 0.2 convert_reduce_fusion
  1.0 0.1 select_reduce_fusion
  1.1 0.1 reshape.113
  1.2 0.6 pad.4.code_ref.meta_ref
  1.9 285.6 %shard_map.46 = (bf16[2,4,32,256]{3,2,1,0:T(8,128)(2,1)}, bf16[8,4,8,256,256]{4,3,2,1,0:T(8,128)(2,1)}) custom-call(s32[32,1,128]{2,1,0:T(1,128)} %pad.4.code_ref.meta_ref, s32[32,1,128]{2,1,0:T(1,128)} %pad.4.code_ref.meta_ref, bf16[32,256,256]{2,1,0:T(8,128)(2,1)} %bitcast.4, bf16[32,256,256]{2,1,0:T(8,128)(2,1)} %bitcast.5, bf16[8,256,256]{2,1,0:T(8,128)(2,1)} %bitcast.6), custom_call_target="tpu_custom_call" | custom-call | tf_op jit(solution)/shard_map/pallas_call | solution.py:252
  287.5 1.6 copy.12
  (2 shorter events, 0.0 us)

commit v4 on v3

--- a/solution.py
+++ b/solution.py
@@ -7,9 +7,17 @@
 
 MESH = pl.DeviceIdType.MESH
 NZ, NY, NX = 8, 4, 4
-STEPS = [(dz, dy) for dy in (0, -1, 1, 2) for dz in (0, 4, 2, -2, 1, -1, 3, -3)]
-ROWS = (0, 1, -1, 2)
-WINDOW = 8
+STEPS = [(dz, dy) for pair in ((0, 2), (-1, 1)) for dz in (0, 4, 3, -3, 2, -2, 1, -1) for dy in pair]
+ROWS = (0, 2, 1, -1)
+NEAR = (0, 1, -1, 2, -2, 3, -3, 4)
+WINDOW = 16
+EARLY = 4
+PLAN = [
+    ("send", 4, 8), ("along", 1), ("table",), ("send", 8, 12), ("hand", 0), ("along", 2), ("send", 12, 16),
+    ("cross", 0), ("hand", 1), ("along", 3), ("send", 16, 20), ("cross", 1), ("hand", 2), ("send", 20, 24),
+    ("group", 0), ("group", 1), ("cross", 2), ("hand", 3), ("send", 24, 28), ("group", 2), ("cross", 3),
+    ("group", 3), ("send", 28, 32), ("group", 4), ("group", 5), ("group", 6), ("group", 7),
+]
 
 
 def slot_rank(dest_row):
@@ -28,11 +36,14 @@
     return lax.rem(index + by + size, size)
 
 
-def contract_all(code_ref, meta_ref, left_ref, right_ref, wave_ref, out_ref, all_ref, send, recv, meta_got, meta_at, stage, halves,
+def contract_all(code_ref, meta_ref, left_hbm, right_hbm, wave_ref, out_ref, all_ref, left_ref, right_ref, send, recv, meta_got, meta_at, stage, halves,
                  picked, acc, pair, half_sum, got, own_sem, stage_sem, a2a_s, a2a_r, meta_s, meta_r, ring_s, ring_r,
-                 row_s, row_r, col_s, col_r, hand_s, hand_r, core_s, core_r, pair_s, pair_r, sum_s, sum_r):
+                 row_s, row_r, near_s, near_r, col_s, col_r, hand_s, hand_r, core_s, core_r, pair_s, pair_r, sum_s, sum_r):
     z, y, x, c = place()
     width = left_ref.shape[-1]
+    left_load = pltpu.make_async_copy(left_hbm, left_ref, own_sem.at[3])
+    left_load.start()
+    right_load = pltpu.make_async_copy(right_hbm, right_ref, own_sem.at[4])
 
     def device(dz=0, dy=0, dx=0, dc=0):
         return (shift(z, dz, NZ) * NY + shift(y, dy, NY), shift(x, dx, NX) * 2 + lax.rem(c + dc, 2))
@@ -55,13 +66,22 @@
     own = pltpu.make_async_copy(wave_ref.at[mine], all_ref.at[mine, y, z], own_sem.at[0])
     own.start()
 
-    ring = {}
+    ring, rows, cols = {}, {}, {}
 
     def ring_step(sign, hop):
         k = hop - 1 + (4 if sign < 0 else 0)
         spot = all_ref.at[mine, y, shift(z, -sign * (hop - 1), NZ)]
         src = wave_ref.at[mine] if hop == 1 else spot
         ring[sign, hop] = remote(src, spot, (ring_s.at[k], ring_r.at[k]), device(dz=sign))
+
+    def spread(dz):
+        spot = all_ref.at[mine, y, shift(z, dz, NZ)]
+        src = spot if dz else wave_ref.at[mine]
+        j = NEAR.index(dz)
+        for i, dx in enumerate((1, -1)):
+            cols[0, i, j] = remote(src, spot, (near_s.at[i, j], near_r.at[i, j]), device(dx=dx))
+        for i, dy in enumerate(ROWS[1:]):
+            rows[i, j] = remote(src, spot, (row_s.at[i, j], row_r.at[i, j]), device(dy=-dy))
 
     a2a = []
     metas = []
@@ -94,52 +114,69 @@
 
     ring_step(1, 1)
     ring_step(-1, 1)
-    for k in range(4):
+    spread(0)
+    left_load.wait()
+    right_load.start()
+    for k in range(EARLY):
         send_left(k)
     for k in range(32):
         send_meta(k)
     acc[...] = jnp.zeros_like(acc)
-    for hop in (2, 3, 4):
-        ring[1, hop - 1].wait_recv()
-        ring_step(1, hop)
-        if hop < 4:
-            ring[-1, hop - 1].wait_recv()
-            ring_step(-1, hop)
-    ring[1, 4].wait_recv()
-    ring[-1, 3].wait_recv()
+    for hop in (1, 2, 3, 4):
+        for sign in (1, -1):
+            if sign > 0 or hop < 4:
+                ring[sign, hop].wait_recv()
+                if hop < (4 if sign > 0 else 3):
+                    ring_step(sign, hop + 1)
+                spread(-sign * hop if hop < 4 else 4)
     own.wait()
-
-    rows, cols, hands, cores = [], [], [], []
-    for i, dy in enumerate(ROWS[1:]):
-        rows.append(remote(all_ref.at[mine, y], all_ref.at[mine, y], (row_s.at[i], row_r.at[i]), device(dy=-dy)))
+    right_load.wait()
+
+    hands, cores = {}, {}
 
     def along(q):
-        if q:
-            rows[q - 1].wait_recv()
         line = shift(y, ROWS[q], NY)
+        for j in range(NZ):
+            rows[q - 1, j].wait_recv()
         for i, dx in enumerate((1, -1)):
             spot = all_ref.at[mine, line]
-            cols.append(remote(spot, spot, (col_s.at[q, i], col_r.at[q, i]), device(dx=dx)))
+            cols[q, i] = remote(spot, spot, (col_s.at[q, i], col_r.at[q, i]), device(dx=dx))
 
     def hand_on(q):
         line = shift(y, ROWS[q], NY)
         for i, dx in enumerate((1, -1)):
-            cols[2 * q + i].wait_recv()
+            if q:
+                cols[q, i].wait_recv()
+            else:
+                for j in range(NZ):
+                    cols[0, i, j].wait_recv()
             spot = all_ref.at[term(-dx), line, pl.ds(4 * i, 4)]
-            hands.append(remote(spot, spot, (hand_s.at[q, i], hand_r.at[q, i]), device(dx=dx)))
+            hands[q, i] = remote(spot, spot, (hand_s.at[q, i], hand_r.at[q, i]), device(dx=dx))
 
     def across(q):
         line = shift(y, ROWS[q], NY)
         for i in range(2):
-            hands[2 * q + i].wait_recv()
+            hands[q, i].wait_recv()
         for dx in range(NX):
             spot = all_ref.at[term(dx), line]
-            cores.append(remote(spot, spot, (core_s.at[q, dx], core_r.at[q, dx]), device(dc=1)))
+            cores[q, dx] = remote(spot, spot, (core_s.at[q, dx], core_r.at[q, dx]), device(dc=1))
+
+    table = []
+
+    def read_table():
+        for copy in metas:
+            copy.wait() if copy is metas[0] else copy.wait_recv()
+        copy = pltpu.make_async_copy(meta_got, meta_at, own_sem.at[2])
+        copy.start()
+        table.append(copy)
 
     def group(g):
-        if g % 2 == 0:
-            for copy in cores[2 * g : 2 * g + 4]:
-                copy.wait_recv()
+        if g == 0:
+            table[0].wait()
+        if g % 4 == 0:
+            for q in (g // 2, g // 2 + 1):
+                for dx in range(NX):
+                    cores[q, dx].wait_recv()
         loads = []
         for i in range(4):
             dz, dy = STEPS[4 * g + i]
@@ -177,37 +214,12 @@
         lax.fori_loop(0, 8, slot, 0)
         lax.fori_loop(0, 4, block, 0)
 
-    along(0)
-    paced(4, 12)
-    for copy in metas:
-        copy.wait() if copy is metas[0] else copy.wait_recv()
-    table = pltpu.make_async_copy(meta_got, meta_at, own_sem.at[2])
-    table.start()
-    along(1)
-    paced(12, 16)
-    along(2)
-    hand_on(0)
-    paced(16, 20)
-    along(3)
-    across(0)
-    hand_on(1)
-    paced(20, 24)
-    across(1)
-    table.wait()
-    group(0)
-    hand_on(2)
-    paced(24, 26)
-    group(1)
-    paced(26, 28)
-    across(2)
-    group(2)
-    hand_on(3)
-    paced(28, 30)
-    group(3)
-    paced(30, 32)
-    across(3)
-    for g in range(4, 8):
-        group(g)
+    def send_on(first, last):
+        paced(max(first, EARLY), last)
+
+    run = dict(send=send_on, table=read_table, along=along, hand=hand_on, cross=across, group=group)
+    for kind, *rest in PLAN:
+        run[kind](*rest)
 
     order = (1, -1, 2, 0)
     pairs, sums = [], []
@@ -224,7 +236,10 @@
         total += got[i].astype(jnp.float32)
     out_ref[...] = total.astype(out_ref.dtype)
 
-    for copy in [*rows, *cols, *hands, *cores, *ring.values(), *metas[1:], *a2a[32 - WINDOW :], *pairs, *sums]:
+    for group_of in (rows, cols, hands, cores, ring):
+        for copy in group_of.values():
+            copy.wait_send()
+    for copy in [*metas[1:], *a2a[max(32 - WINDOW, 1) :], *pairs, *sums]:
         copy.wait_send()
 
 
@@ -255,9 +270,11 @@
             jax.ShapeDtypeStruct(piece, low),
             jax.ShapeDtypeStruct((terms, NY, NZ, *block), low),
         ),
-        in_specs=[pl.BlockSpec(memory_space=pltpu.SMEM), vmem, vmem, vmem, hbm],
+        in_specs=[pl.BlockSpec(memory_space=pltpu.SMEM), vmem, hbm, hbm, hbm],
         out_specs=(vmem, hbm),
         scratch_shapes=[
+            pltpu.VMEM((per_dev, *block), low),
+            pltpu.VMEM((per_dev, *block), low),
             pltpu.VMEM((sectors, capacity, *block), low),
             pltpu.VMEM((sectors, capacity, *block), low),
             pltpu.VMEM((sectors, 1, 128), jnp.int32),
@@ -269,8 +286,8 @@
             pltpu.VMEM((NX, *piece), wide),
             pltpu.VMEM((3, *piece), low),
             pltpu.VMEM((3, *piece), low),
-            dma((3,)), dma((4,)),
-            dma((32,)), dma((32,)), dma((32,)), dma((32,)), dma((8,)), dma((8,)), dma((3,)), dma((3,)),
+            dma((5,)), dma((4,)),
+            dma((32,)), dma((32,)), dma((32,)), dma((32,)), dma((8,)), dma((8,)), dma((3, 8)), dma((3, 8)), dma((2, 8)), dma((2, 8)),
             dma((4, 2)), dma((4, 2)), dma((4, 2)), dma((4, 2)), dma((4, 4)), dma((4, 4)),
             dma((4,)), dma((4,)), dma((3,)), dma((3,)),
         ],

time: 289 us -> 245 us (0.85)
  the two profiles are of different devices: /device:TPU:243 before, /device:TPU:1 now
where the time goes in v4:
time: 245 us
  Pallas kernels  241 us (98%)
  local copies, waits for them, and re-layouts  3.13 us (1%)
    pallas_call x1, Pallas kernels, shards(): pl.pallas_call(contract_all, out_shape=(jax.ShapeDtypeStruct(piece, low),...  241 us

profile of v4, /device:TPU:1, one launch (start us, length us, event | category | flops | bytes accessed | tf_op | source)
XLA Modules:
  0.0 244.9 jit_solution(5393551547558283001)
XLA Ops:
  0.0 0.8 copy.9
  0.8 0.1 reshape.112
  0.9 0.2 convert_reduce_fusion
  1.0 0.1 select_reduce_fusion
  1.1 0.1 reshape.113
  1.2 0.6 pad.4.code_ref.meta_ref
  1.9 241.5 %shard_map.46 = (bf16[2,4,32,256]{3,2,1,0:T(8,128)(2,1)}, bf16[8,4,8,256,256]{4,3,2,1,0:T(8,128)(2,1)}) custom-call(s32[32,1,128]{2,1,0:T(1,128)} %pad.4.code_ref.meta_ref, s32[32,1,128]{2,1,0:T(1,128)} %pad.4.code_ref.meta_ref, bf16[32,256,256]{2,1,0:T(8,128)(2,1)} %bitcast.4, bf16[32,256,256]{2,1,0:T(8,128)(2,1)} %bitcast.5, bf16[8,256,256]{2,1,0:T(8,128)(2,1)} %bitcast.6), custom_call_target="tpu_custom_call" | custom-call | tf_op jit(solution)/shard_map/pallas_call | solution.py:267
  243.4 1.6 copy.12
  (2 shorter events, 0.0 us)

commit v5 on v4

--- a/solution.py
+++ b/solution.py
@@ -12,8 +12,10 @@
 NEAR = (0, 1, -1, 2, -2, 3, -3, 4)
 WINDOW = 16
 EARLY = 4
+SLOT_UNROLL = 4
+BLOCK_UNROLL = 2
 PLAN = [
-    ("send", 4, 8), ("along", 1), ("table",), ("send", 8, 12), ("hand", 0), ("along", 2), ("send", 12, 16),
+    ("send", 0, 8), ("along", 1), ("table",), ("send", 8, 12), ("hand", 0), ("along", 2), ("send", 12, 16),
     ("cross", 0), ("hand", 1), ("along", 3), ("send", 16, 20), ("cross", 1), ("hand", 2), ("send", 20, 24),
     ("group", 0), ("group", 1), ("cross", 2), ("hand", 3), ("send", 24, 28), ("group", 2), ("cross", 3),
     ("group", 3), ("send", 28, 32), ("group", 4), ("group", 5), ("group", 6), ("group", 7),
@@ -36,7 +38,7 @@
     return lax.rem(index + by + size, size)
 
 
-def contract_all(code_ref, meta_ref, left_hbm, right_hbm, wave_ref, out_ref, all_ref, left_ref, right_ref, send, recv, meta_got, meta_at, stage, halves,
+def contract_all(code_ref, meta_ref, left_hbm, right_hbm, wave_ref, out_ref, all_ref, left_ref, right_ref, send, recv, meta_got, meta_at, stage_even, stage_odd, halves,
                  picked, acc, pair, half_sum, got, own_sem, stage_sem, a2a_s, a2a_r, meta_s, meta_r, ring_s, ring_r,
                  row_s, row_r, near_s, near_r, col_s, col_r, hand_s, hand_r, core_s, core_r, pair_s, pair_r, sum_s, sum_r):
     z, y, x, c = place()
@@ -55,6 +57,19 @@
     partners = [device(dz, dy) for dz, dy in STEPS[1:]] + [device(dx=dx) for dx in (1, -1, 2)] + [device(dc=1)]
     for partner in partners:
         pl.semaphore_signal(barrier, inc=1, device_id=partner, device_id_type=MESH)
+
+    def owner_of(k):
+        dz, dy = STEPS[k]
+        return shift(z, dz, NZ) * NY + shift(y, dy, NY)
+
+    def pack(k):
+        buf = recv if k == 0 else send
+        for r in range(2):
+            buf[k, r] = left_ref[code_ref[owner_of(k), 0, r] // 8]
+
+    left_load.wait()
+    for k in range(EARLY):
+        pack(k)
     pl.semaphore_wait(barrier, len(partners))
 
     def remote(src, dst, sems, where):
@@ -86,10 +101,6 @@
     a2a = []
     metas = []
 
-    def owner_of(k):
-        dz, dy = STEPS[k]
-        return shift(z, dz, NZ) * NY + shift(y, dy, NY)
-
     def send_meta(k):
         src, dst = meta_ref.at[owner_of(k)], meta_got.at[k]
         if k == 0:
@@ -100,10 +111,8 @@
         metas.append(copy)
 
     def send_left(k):
-        to = owner_of(k)
-        buf = recv if k == 0 else send
-        for r in range(2):
-            buf[k, r] = left_ref[code_ref[to, 0, r] // 8]
+        if k >= EARLY:
+            pack(k)
         a2a.append(k and remote(send.at[k], recv.at[k], (a2a_s.at[k], a2a_r.at[k]), device(*STEPS[k])))
 
     def paced(first, last):
@@ -115,13 +124,9 @@
     ring_step(1, 1)
     ring_step(-1, 1)
     spread(0)
-    left_load.wait()
     right_load.start()
     for k in range(EARLY):
         send_left(k)
-    for k in range(32):
-        send_meta(k)
-    acc[...] = jnp.zeros_like(acc)
     for hop in (1, 2, 3, 4):
         for sign in (1, -1):
             if sign > 0 or hop < 4:
@@ -130,9 +135,14 @@
                     ring_step(sign, hop + 1)
                 spread(-sign * hop if hop < 4 else 4)
     own.wait()
-    right_load.wait()
+    for k in range(32):
+        send_meta(k)
 
     hands, cores = {}, {}
+
+    def over(q, dx):
+        spot = all_ref.at[term(dx), shift(y, ROWS[q], NY)]
+        cores[q, dx] = remote(spot, spot, (core_s.at[q, dx % NX], core_r.at[q, dx % NX]), device(dc=1))
 
     def along(q):
         line = shift(y, ROWS[q], NY)
@@ -141,6 +151,7 @@
         for i, dx in enumerate((1, -1)):
             spot = all_ref.at[mine, line]
             cols[q, i] = remote(spot, spot, (col_s.at[q, i], col_r.at[q, i]), device(dx=dx))
+        over(q, 0)
 
     def hand_on(q):
         line = shift(y, ROWS[q], NY)
@@ -152,14 +163,14 @@
                     cols[0, i, j].wait_recv()
             spot = all_ref.at[term(-dx), line, pl.ds(4 * i, 4)]
             hands[q, i] = remote(spot, spot, (hand_s.at[q, i], hand_r.at[q, i]), device(dx=dx))
+            over(q, -dx)
+        if q == 0:
+            over(q, 0)
 
     def across(q):
-        line = shift(y, ROWS[q], NY)
         for i in range(2):
             hands[q, i].wait_recv()
-        for dx in range(NX):
-            spot = all_ref.at[term(dx), line]
-            cores[q, dx] = remote(spot, spot, (core_s.at[q, dx], core_r.at[q, dx]), device(dc=1))
+        over(q, 2)
 
     table = []
 
@@ -170,21 +181,32 @@
         copy.start()
         table.append(copy)
 
+    ready, loads = set(), {}
+    stages = (stage_even, stage_odd)
+
+    def fetch(g):
+        for q in (0, 1) if g < 4 else (2, 3):
+            if q not in ready:
+                ready.add(q)
+                for dx in (0, 1, -1, 2):
+                    cores[q, dx].wait_recv()
+        for i in range(4):
+            dz, dy = STEPS[4 * g + i]
+            spot = all_ref.at[:, shift(y, -dy, NY), shift(z, -dz, NZ)]
+            loads[g, i] = pltpu.make_async_copy(spot, stages[g % 2].at[i], stage_sem.at[g % 2, i])
+            loads[g, i].start()
+
     def group(g):
         if g == 0:
             table[0].wait()
-        if g % 4 == 0:
-            for q in (g // 2, g // 2 + 1):
-                for dx in range(NX):
-                    cores[q, dx].wait_recv()
-        loads = []
+            right_load.wait()
+            acc[...] = jnp.zeros_like(acc)
+        if (g, 0) not in loads:
+            fetch(g)
         for i in range(4):
-            dz, dy = STEPS[4 * g + i]
-            copy = pltpu.make_async_copy(all_ref.at[:, shift(y, -dy, NY), shift(z, -dz, NZ)], stage.at[i], stage_sem.at[i])
-            copy.start()
-            loads.append(copy)
-        for copy in loads:
-            copy.wait()
+            loads[g, i].wait()
+        if g not in (3, 7):
+            fetch(g + 1)
         for k in range(max(4 * g, 1), 4 * g + 4):
             a2a[k].wait_recv()
 
@@ -195,7 +217,7 @@
             left = recv[4 * g + i, r]
             span = pl.ds(pl.multiple_of(j * width, width), width)
             for v in range(2):
-                half = jnp.dot(left, stage[i, v * 4 + source], preferred_element_type=jnp.float32)
+                half = jnp.dot(left, stages[g % 2][i, v * 4 + source], preferred_element_type=jnp.float32)
                 halves[v * width : (v + 1) * width, span] = half.astype(halves.dtype)
             right = right_ref[code // 32 * 4 + owner]
             for b in range(4):
@@ -211,8 +233,8 @@
                     acc[t % 2, t // 2, v, b] += product[at : at + 32]
             return carry
 
-        lax.fori_loop(0, 8, slot, 0)
-        lax.fori_loop(0, 4, block, 0)
+        lax.fori_loop(0, 8, slot, 0, unroll=SLOT_UNROLL)
+        lax.fori_loop(0, 4, block, 0, unroll=BLOCK_UNROLL)
 
     def send_on(first, last):
         paced(max(first, EARLY), last)
@@ -280,13 +302,14 @@
             pltpu.VMEM((sectors, 1, 128), jnp.int32),
             pltpu.SMEM((sectors, 1, 128), jnp.int32),
             pltpu.VMEM((4, terms, *block), low),
+            pltpu.VMEM((4, terms, *block), low),
             pltpu.VMEM((2 * width, 8 * width), low),
             pltpu.VMEM((4, 8 * width, width), low),
             pltpu.VMEM((2, NX, *piece), wide),
             pltpu.VMEM((NX, *piece), wide),
             pltpu.VMEM((3, *piece), low),
             pltpu.VMEM((3, *piece), low),
-            dma((5,)), dma((4,)),
+            dma((5,)), dma((2, 4)),
             dma((32,)), dma((32,)), dma((32,)), dma((32,)), dma((8,)), dma((8,)), dma((3, 8)), dma((3, 8)), dma((2, 8)), dma((2, 8)),
             dma((4, 2)), dma((4, 2)), dma((4, 2)), dma((4, 2)), dma((4, 4)), dma((4, 4)),
             dma((4,)), dma((4,)), dma((3,)), dma((3,)),

time: 245 us -> 240 us (0.980)
  Pallas kernels: 241 us -> 237 us
    pallas_call x1, Pallas kernels: 241 us -> 237 us  [shards(): pl.pallas_call(contract_all, out_shape=(jax.ShapeDtypeStruct(piece, low),...]
where the time goes in v5:
time: 240 us
  Pallas kernels  237 us (99%)
  local copies, waits for them, and re-layouts  3.13 us (1%)
    pallas_call x1, Pallas kernels, shards(): pl.pallas_call(contract_all, out_shape=(jax.ShapeDtypeStruct(piece, low),...  237 us

profile of v5, /device:TPU:1, one launch (start us, length us, event | category | flops | bytes accessed | tf_op | source)
XLA Modules:
  0.0 240.1 jit_solution(17924990366219960398)
XLA Ops:
  0.0 0.8 copy.9
  0.8 0.1 reshape.112
  0.9 0.2 convert_reduce_fusion
  1.0 0.1 select_reduce_fusion
  1.1 0.1 reshape.113
  1.2 0.6 pad.4.code_ref.meta_ref
  1.9 236.6 %shard_map.46 = (bf16[2,4,32,256]{3,2,1,0:T(8,128)(2,1)}, bf16[8,4,8,256,256]{4,3,2,1,0:T(8,128)(2,1)}) custom-call(s32[32,1,128]{2,1,0:T(1,128)} %pad.4.code_ref.meta_ref, s32[32,1,128]{2,1,0:T(1,128)} %pad.4.code_ref.meta_ref, bf16[32,256,256]{2,1,0:T(8,128)(2,1)} %bitcast.4, bf16[32,256,256]{2,1,0:T(8,128)(2,1)} %bitcast.5, bf16[8,256,256]{2,1,0:T(8,128)(2,1)} %bitcast.6), custom_call_target="tpu_custom_call" | custom-call | tf_op jit(solution)/shard_map/pallas_call | solution.py:289
  238.5 1.6 copy.12
  (2 shorter events, 0.0 us)

commit v6 on v5

--- a/solution.py
+++ b/solution.py
@@ -234,7 +234,21 @@
             return carry
 
         lax.fori_loop(0, 8, slot, 0, unroll=SLOT_UNROLL)
-        lax.fori_loop(0, 4, block, 0, unroll=BLOCK_UNROLL)
+        if g < 7:
+            lax.fori_loop(0, 4, block, 0, unroll=BLOCK_UNROLL)
+            return
+        for half in range(2):
+            lax.fori_loop(2 * half, 2 * half + 2, block, 0, unroll=BLOCK_UNROLL)
+            send_pairs(half)
+
+    order = (1, -1, 2, 0)
+    pairs, sums = {}, {}
+
+    def send_pairs(half):
+        part = pl.ds(2 * half, 2)
+        for i, dx in enumerate(order):
+            src, dst = acc.at[1 - c, shift(x, dx, NX), :, part], pair.at[i, :, part]
+            pairs[i, half] = remote(src, dst, (pair_s.at[i, half], pair_r.at[i, half]), device(dc=1))
 
     def send_on(first, last):
         paced(max(first, EARLY), last)
@@ -243,25 +257,28 @@
     for kind, *rest in PLAN:
         run[kind](*rest)
 
-    order = (1, -1, 2, 0)
-    pairs, sums = [], []
-    for i, dx in enumerate(order):
-        pairs.append(remote(acc.at[1 - c, shift(x, dx, NX)], pair.at[i], (pair_s.at[i], pair_r.at[i]), device(dc=1)))
-    for i, dx in enumerate(order[:3]):
-        pairs[i].wait_recv()
-        half_sum[i] = (acc[c, shift(x, dx, NX)] + pair[i]).astype(half_sum.dtype)
-        sums.append(remote(half_sum.at[i], got.at[i], (sum_s.at[i], sum_r.at[i]), device(dx=dx)))
-    pairs[3].wait_recv()
-    total = acc[c, x] + pair[3]
-    for i in range(3):
-        sums[i].wait_recv()
-        total += got[i].astype(jnp.float32)
-    out_ref[...] = total.astype(out_ref.dtype)
-
-    for group_of in (rows, cols, hands, cores, ring):
+    for half in range(2):
+        part = slice(2 * half, 2 * half + 2)
+        for i, dx in enumerate(order[:3]):
+            pairs[i, half].wait_recv()
+            both = acc[c, shift(x, dx, NX), :, part] + pair[i, :, part]
+            half_sum[i, :, part] = both.astype(half_sum.dtype)
+            spot = pl.ds(2 * half, 2)
+            src, dst = half_sum.at[i, :, spot], got.at[i, :, spot]
+            sums[i, half] = remote(src, dst, (sum_s.at[i, half], sum_r.at[i, half]), device(dx=dx))
+    for half in range(2):
+        part = slice(2 * half, 2 * half + 2)
+        pairs[3, half].wait_recv()
+        total = acc[c, x, :, part] + pair[3, :, part]
+        for i in range(3):
+            sums[i, half].wait_recv()
+            total += got[i, :, part].astype(jnp.float32)
+        out_ref[:, part] = total.astype(out_ref.dtype)
+
+    for group_of in (rows, cols, hands, cores, ring, pairs, sums):
         for copy in group_of.values():
             copy.wait_send()
-    for copy in [*metas[1:], *a2a[max(32 - WINDOW, 1) :], *pairs, *sums]:
+    for copy in [*metas[1:], *a2a[max(32 - WINDOW, 1) :]]:
         copy.wait_send()
 
 
@@ -312,7 +329,7 @@
             dma((5,)), dma((2, 4)),
             dma((32,)), dma((32,)), dma((32,)), dma((32,)), dma((8,)), dma((8,)), dma((3, 8)), dma((3, 8)), dma((2, 8)), dma((2, 8)),
             dma((4, 2)), dma((4, 2)), dma((4, 2)), dma((4, 2)), dma((4, 4)), dma((4, 4)),
-            dma((4,)), dma((4,)), dma((3,)), dma((3,)),
+            dma((4, 2)), dma((4, 2)), dma((3, 2)), dma((3, 2)),
         ],
         compiler_params=pltpu.CompilerParams(
             collective_id=0, has_side_effects=True, vmem_limit_bytes=56 << 20

time: 240 us -> 240 us (level)
  no operation moved by 1% of the time
where the time goes in v6:
time: 240 us; the launch traced here: 239 us
  Pallas kernels  236 us (98%)
  local copies, waits for them, and re-layouts  3.13 us (1%)
    pallas_call x1, Pallas kernels, shards(): pl.pallas_call(contract_all, out_shape=(jax.ShapeDtypeStruct(piece, low),...  236 us

profile of v6, /device:TPU:1, one launch (start us, length us, event | category | flops | bytes accessed | tf_op | source)
XLA Modules:
  0.0 239.5 jit_solution(8086500683453468720)
XLA Ops:
  0.0 0.8 copy.9
  0.8 0.1 reshape.112
  0.9 0.2 convert_reduce_fusion
  1.0 0.1 select_reduce_fusion
  1.1 0.1 reshape.113
  1.2 0.6 pad.4.code_ref.meta_ref
  1.9 236.0 %shard_map.46 = (bf16[2,4,32,256]{3,2,1,0:T(8,128)(2,1)}, bf16[8,4,8,256,256]{4,3,2,1,0:T(8,128)(2,1)}) custom-call(s32[32,1,128]{2,1,0:T(1,128)} %pad.4.code_ref.meta_ref, s32[32,1,128]{2,1,0:T(1,128)} %pad.4.code_ref.meta_ref, bf16[32,256,256]{2,1,0:T(8,128)(2,1)} %bitcast.4, bf16[32,256,256]{2,1,0:T(8,128)(2,1)} %bitcast.5, bf16[8,256,256]{2,1,0:T(8,128)(2,1)} %bitcast.6), custom_call_target="tpu_custom_call" | custom-call | tf_op jit(solution)/shard_map/pallas_call | solution.py:306
  237.9 1.6 copy.12
  (2 shorter events, 0.0 us)
